TPU v7x, 512 devices: a whole 4x8x8 slice. The times are simulated.
512 devices in a mesh: dp: 8 (over z), expert: 64 (over x, y, core).
Axes of the slice: x: 4, y: 8, z: 8, core: 2. Of those that a mesh axis runs over, the one named last changes fastest.
Arguments:
- tokens: bfloat16 [2048, 2048], P('expert', 'dp'), may hold values from -6 to 6
- cotangent: bfloat16 [2048, 2048], P('expert', 'dp'), may hold values from -6 to 6
- routes: int32 [2048, 8], P('expert'), may hold values from 0 to 63, all different within a row; in each aligned block of 32 rows (0 to 31, 32 to 63, ...) at most 5 rows name the same one
- probs: float32 [2048, 8], P('expert'), may hold values from 0.03 to 0.6
- matching: int32 [64], replicated, may hold values from 0 to 63, as said below
- gate_weight: bfloat16 [64, 2048, 1024], P('expert', None, 'dp'), may hold values from -0.125 to 0.125
- up_weight: bfloat16 [64, 2048, 1024], P('expert', None, 'dp'), may hold values from -0.125 to 0.125
- down_weight: bfloat16 [64, 2048, 1024], P('expert', None, 'dp'), may hold values from -0.1875 to 0.1875
Outputs:
- input_grad: bfloat16 [2048, 2048], P('expert', 'dp')
- gate_weight_grad: float32 [64, 2048, 1024], P('expert', None, 'dp')
- up_weight_grad: float32 [64, 2048, 1024], P('expert', None, 'dp')
- down_weight_grad: float32 [64, 2048, 1024], P('expert', None, 'dp')
Inputs may be any that keep to these rules, and one draw needn't show every extreme that they name: matching pairs the experts: matching[matching[i]] == i and matching[i] != i. `routes`: each token names 8 different experts; within each aligned block of 32 tokens no expert is named by more than 5 tokens.
All inputs are finite; a program needn't handle non-finite values.
Results may differ from a plain program's by a relative error of at most 0.015.
Values may be sent and summed in bfloat16 or wider, within the bound.
No kernel may reach another device: no remote copies, remote signals or barrier semaphores. Data moves between devices by JAX's collectives and lax.ppermute only.
A program may use at most 64 MiB of HBM per device.

v0:
```python
import jax
import jax.numpy as jnp
from jax import lax
from jax.sharding import PartitionSpec as P

contract_rows = (((0,), (0,)), ((), ()))
contract_cols = (((1,), (1,)), ((), ()))


def relay_weights(first, second, third):
    return (
        lax.all_to_all(first, "expert", split_axis=1, concat_axis=0, tiled=True),
        lax.all_to_all(second, "expert", split_axis=1, concat_axis=0, tiled=True),
        lax.all_to_all(third, "expert", split_axis=1, concat_axis=0, tiled=True),
    )


def migrate(arrays, matching, mover):
    experts = matching.shape[0]
    model_width = arrays[0].shape[-2]
    hidden_width = arrays[0].shape[-1]
    piece_rows = model_width // experts
    split = [a.reshape(1, experts, piece_rows, hidden_width) for a in arrays]
    spread = mover(split[0], split[1], split[2])
    ordered = [
        jnp.take(s, matching, axis=0).reshape(1, experts, piece_rows, hidden_width) for s in spread
    ]
    landed = mover(ordered[0], ordered[1], ordered[2])
    return [w.reshape(model_width, hidden_width) for w in landed]


def layout(routes, probs, target_table, capacity):
    experts = target_table.shape[0]
    tok_rows = routes.shape[0]
    top_count = routes.shape[1]
    pair_count = tok_rows * top_count
    pair_expert = routes.reshape(pair_count)
    onehot = (pair_expert[:, None] == jnp.arange(experts, dtype=jnp.int32)[None, :]).astype(
        jnp.int32
    )
    running = jnp.cumsum(onehot, axis=0)
    rank = jnp.sum(onehot * running, axis=1) - 1
    target = jnp.sum(onehot * target_table[None, :], axis=1)
    slot = target * capacity + rank
    slot_total = experts * capacity
    owners = jnp.arange(pair_count, dtype=jnp.int32) // top_count
    slot_token = jnp.full((slot_total,), tok_rows, jnp.int32).at[slot].set(owners)
    slot_prob = jnp.zeros((slot_total,), jnp.float32).at[slot].set(probs.reshape(pair_count))
    return (slot, slot_token, slot_prob)


def build_rows(tokens, cotangent, slot_token, slot_prob):
    blank = jnp.zeros((1, tokens.shape[1]), jnp.bfloat16)
    inputs = jnp.take(jnp.concatenate([tokens, blank], axis=0), slot_token, axis=0)
    picked = jnp.take(jnp.concatenate([cotangent, blank], axis=0), slot_token, axis=0)
    grads = (picked.astype(jnp.float32) * slot_prob[:, None]).astype(jnp.bfloat16)
    return (inputs, grads)


def combine_pairs(returned, slot, tok_rows, top_count):
    rows = jnp.take(returned, slot, axis=0)
    return jnp.sum(rows.reshape(tok_rows, top_count, returned.shape[1]), axis=1)


def expert_grads(inputs, grads, w_gate, w_up, w_down):
    gate = jnp.dot(inputs, w_gate, preferred_element_type=jnp.float32)
    upper = jnp.dot(inputs, w_up, preferred_element_type=jnp.float32)
    sig = jax.nn.sigmoid(gate)
    hidden = (gate * sig * upper).astype(jnp.bfloat16)
    hidden_back = jnp.dot(grads, w_down, preferred_element_type=jnp.float32)
    up_back = (hidden_back * gate * sig).astype(jnp.bfloat16)
    gate_back = (hidden_back * upper * sig * (1.0 + gate * (1.0 - sig))).astype(jnp.bfloat16)
    gate_sum = lax.dot_general(inputs, gate_back, contract_rows, preferred_element_type=jnp.float32)
    up_sum = lax.dot_general(inputs, up_back, contract_rows, preferred_element_type=jnp.float32)
    down_sum = lax.dot_general(grads, hidden, contract_rows, preferred_element_type=jnp.float32)
    return (gate_sum, up_sum, down_sum, gate_back, up_back)


def slice_back(gate_back, up_back, w_gate, w_up):
    first = lax.dot_general(gate_back, w_gate, contract_cols, preferred_element_type=jnp.float32)
    return first + lax.dot_general(up_back, w_up, contract_cols, preferred_element_type=jnp.float32)


def local(tokens, cotangent, routes, probs, matching, gate_weight, up_weight, down_weight):
    experts = matching.shape[0]
    tok_rows = routes.shape[0]
    top_count = routes.shape[1]
    capacity = max(2, 5 * tok_rows * top_count // (4 * experts))
    model_width = gate_weight.shape[1]
    hidden_width = gate_weight.shape[2]
    w_gate, w_up, w_down = migrate((gate_weight, up_weight, down_weight), matching, relay_weights)
    slot, slot_token, slot_prob = layout(routes, probs, matching, capacity)
    whole_in, whole_out = (
        lax.all_gather(tokens, "dp", axis=1, tiled=True),
        lax.all_gather(cotangent, "dp", axis=1, tiled=True),
    )
    inputs, grads = build_rows(whole_in, whole_out, slot_token, slot_prob)
    arrived_in, arrived_out = (
        lax.all_to_all(inputs, "expert", split_axis=0, concat_axis=0, tiled=True),
        lax.all_to_all(grads, "expert", split_axis=0, concat_axis=0, tiled=True),
    )
    gate_sum, up_sum, down_sum, gate_back, up_back = expert_grads(
        arrived_in, arrived_out, w_gate, w_up, w_down
    )
    partial_value = slice_back(gate_back, up_back, w_gate, w_up).astype(jnp.bfloat16)
    pair_back = lax.psum_scatter(partial_value, "dp", scatter_dimension=1, tiled=True).astype(
        jnp.float32
    )
    returned = lax.all_to_all(
        pair_back.astype(jnp.bfloat16), "expert", split_axis=0, concat_axis=0, tiled=True
    ).astype(pair_back.dtype)
    token_sum = combine_pairs(returned, slot, tok_rows, top_count)
    return (
        token_sum.astype(jnp.bfloat16),
        gate_sum.reshape(1, model_width, hidden_width),
        up_sum.reshape(1, model_width, hidden_width),
        down_sum.reshape(1, model_width, hidden_width),
    )


def solution(mesh):
    placed = (
        P("expert", "dp"),
        P("expert", "dp"),
        P("expert", None),
        P("expert", None),
        P(),
        P("expert", None, "dp"),
        P("expert", None, "dp"),
        P("expert", None, "dp"),
    )
    return jax.shard_map(
        local,
        mesh=mesh,
        in_specs=placed,
        out_specs=(
            P("expert", "dp"),
            P("expert", None, "dp"),
            P("expert", None, "dp"),
            P("expert", None, "dp"),
        ),
        check_vma=False,
    )
```

profile of v0, /device:TPU:1, one launch (start us, length us, event | category | flops | bytes accessed | tf_op | source)
XLA Modules:
  0.0 365.6 jit_solution(9097960822106262097)
XLA Ops:
  7.2 29.1 %all_to_all.96 = bf16[1,64,32,128]{3,2,0,1:T(8,128)(2,1)S(1)} all-to-all(bf16[1,64,32,128]{3,2,0,1:T(8,128)(2,1)} %bitcast.85), channel_id=1, replica_groups=mesh['dp'=8,'expert'=64] {'expert'}, dimensions={1} | all-to-all | bytes 1048576 | tf_op jit(solution)/shard_map/all_to_all | solution.py:13
  36.3 23.5 %all_to_all.97 = bf16[1,64,32,128]{3,2,0,1:T(8,128)(2,1)S(1)} all-to-all(bf16[1,64,32,128]{3,2,0,1:T(8,128)(2,1)S(1)} %bitcast.86), channel_id=1, replica_groups=mesh['dp'=8,'expert'=64] {'expert'}, dimensions={1} | all-to-all | bytes 1048576 | tf_op jit(solution)/shard_map/all_to_all | solution.py:12
  59.8 6.3 %all-to-all-start.1 = ((bf16[1,64,32,128]{3,2,0,1:T(8,128)(2,1)}), bf16[1,64,32,128]{3,2,0,1:T(8,128)(2,1)S(1)}, u32[]{:S(2)}, u32[]{:S(2)}) async-start(bf16[1,64,32,128]{3,2,0,1:T(8,128)(2,1)} %bitcast.3), calls=%async_computation.1 | async-start | bytes 1048576 | tf_op jit(solution)/shard_map/all_to_all | solution.py:14
  66.1 0.1 copy.16
  66.2 0.1 eq.25
  66.3 0.1 eq.29
  66.4 0.7 gather_fusion.4
  67.1 0.7 gather_fusion.5
  67.7 15.7 %all-to-all-done.1 = bf16[1,64,32,128]{3,2,0,1:T(8,128)(2,1)S(1)} async-done(((bf16[1,64,32,128]{3,2,0,1:T(8,128)(2,1)}), bf16[1,64,32,128]{3,2,0,1:T(8,128)(2,1)S(1)}, u32[]{:S(2)}, u32[]{:S(2)}) %all-to-all-start.1) | async-done | bytes 524320 | tf_op jit(solution)/shard_map/all_to_all | solution.py:14
  83.4 0.7 gather_fusion.2
  84.1 1.4 fusion.2
  85.4 6.4 %all-to-all-start.7 = ((bf16[1,64,32,128]{3,2,0,1:T(8,128)(2,1)}), bf16[1,64,32,128]{3,2,0,1:T(8,128)(2,1)S(1)}, u32[]{:S(2)}, u32[]{:S(2)}) async-start(bf16[1,64,32,128]{3,2,0,1:T(8,128)(2,1)} %get-tuple-element.11), calls=%async_computation.7 | async-start | bytes 1048576 | tf_op jit(solution)/shard_map/all_to_all | solution.py:12
  91.8 0.6 reduce-window.6
  92.5 0.2 slice_reduce_fusion
  92.7 26.1 %all_gather.7 = bf16[32,2048]{1,0:T(8,128)(2,1)S(1)} all-gather(bf16[32,256]{1,0:T(8,128)(2,1)S(1)} %copy-done.8), channel_id=1, replica_groups=mesh['dp'=8,'expert'=64] {'dp'}, dimensions={1}, use_global_device_ids=true | all-gather | bytes 147456 | tf_op jit(solution)/shard_map/all_gather | solution.py:94
  118.8 0.1 select_reduce_fusion
  118.9 0.6 copy-done.10
  119.5 1.4 scatter_custom_fusion
  120.9 0.0 copy-start
  120.9 15.2 %all-to-all-start.5 = ((bf16[1,64,32,128]{3,2,0,1:T(8,128)(2,1)}), bf16[1,64,32,128]{3,2,0,1:T(8,128)(2,1)S(1)}, u32[]{:S(2)}, u32[]{:S(2)}) async-start(bf16[1,64,32,128]{3,2,0,1:T(8,128)(2,1)} %get-tuple-element.10), calls=%async_computation.5 | async-start | bytes 1048576 | tf_op jit(solution)/shard_map/all_to_all | solution.py:13
  136.1 2.4 gather_fusion.3
  138.6 0.2 broadcast_select_fusion
  138.8 1.6 all_to_all.76
  140.4 13.0 %all-to-all-done.5 = bf16[1,64,32,128]{3,2,0,1:T(8,128)(2,1)S(1)} async-done(((bf16[1,64,32,128]{3,2,0,1:T(8,128)(2,1)}), bf16[1,64,32,128]{3,2,0,1:T(8,128)(2,1)S(1)}, u32[]{:S(2)}, u32[]{:S(2)}) %all-to-all-start.5) | async-done | bytes 524320 | tf_op jit(solution)/shard_map/all_to_all | solution.py:13
  153.4 0.8 copy-done.2
  154.2 6.3 %all-to-all-start.3 = ((bf16[64,5,2048]{2,1,0:T(8,128)(2,1)}), bf16[64,5,2048]{2,1,0:T(8,128)(2,1)S(1)}, u32[]{:S(2)}, u32[]{:S(2)}) async-start(bf16[64,5,2048]{2,1,0:T(8,128)(2,1)} %all_to_all.76), calls=%async_computation.3 | async-start | bytes 4194304 | tf_op jit(solution)/shard_map/all_to_all | solution.py:99
  160.5 20.2 %all_gather.6 = bf16[32,2048]{1,0:T(8,128)(2,1)S(1)} all-gather(bf16[32,256]{1,0:T(8,128)(2,1)S(1)} %copy-done.9), channel_id=1, replica_groups=mesh['dp'=8,'expert'=64] {'dp'}, dimensions={1}, use_global_device_ids=true | all-gather | bytes 147456 | tf_op jit(solution)/shard_map/all_gather | solution.py:95
  180.8 3.0 gather_fusion.1
  183.8 0.1 copy.19
  183.9 0.1 reshape.244
  184.0 1.6 scatter_custom_fusion.1
  185.6 1.7 multiply_convert_fusion
  187.3 1.6 all_to_all.70
  188.9 22.9 %all-to-all-done.3 = bf16[64,5,2048]{2,1,0:T(8,128)(2,1)S(1)} async-done(((bf16[64,5,2048]{2,1,0:T(8,128)(2,1)}), bf16[64,5,2048]{2,1,0:T(8,128)(2,1)S(1)}, u32[]{:S(2)}, u32[]{:S(2)}) %all-to-all-start.3) | async-done | bytes 1310752 | tf_op jit(solution)/shard_map/all_to_all | solution.py:99
  211.8 57.2 %all_to_all.98 = bf16[64,5,2048]{2,1,0:T(8,128)(2,1)} all-to-all(bf16[64,5,2048]{2,1,0:T(8,128)(2,1)} %all_to_all.70), channel_id=1, replica_groups=mesh['dp'=8,'expert'=64] {'expert'}, dimensions={0} | all-to-all | bytes 2621440 | tf_op jit(solution)/shard_map/all_to_all | solution.py:100
  268.9 6.0 %all-to-all-start.2 = ((bf16[1,64,32,128]{3,2,0,1:T(8,128)(2,1)}), bf16[1,64,32,128]{3,2,0,1:T(8,128)(2,1)}, u32[]{:S(2)}, u32[]{:S(2)}) async-start(bf16[1,64,32,128]{3,2,0,1:T(8,128)(2,1)} %get-tuple-element.12), calls=%async_computation.2 | async-start | bytes 1048576 | tf_op jit(solution)/shard_map/all_to_all | solution.py:14
  274.9 0.0 reduce-scatter.2.cloned.1.call-start
  275.0 0.6 all_to_all.78
  275.6 0.0 copy-start.1
  275.6 2.6 all_to_all.72
  278.2 0.5 fusion.15
  278.7 0.5 copy-done.3
  279.3 0.5 fusion.14
  279.8 12.4 %all-to-all-done.2 = bf16[1,64,32,128]{3,2,0,1:T(8,128)(2,1)} async-done(((bf16[1,64,32,128]{3,2,0,1:T(8,128)(2,1)}), bf16[1,64,32,128]{3,2,0,1:T(8,128)(2,1)}, u32[]{:S(2)}, u32[]{:S(2)}) %all-to-all-start.2) | async-done | bytes 524320 | tf_op jit(solution)/shard_map/all_to_all | solution.py:14
  292.2 1.5 multiply_convert_fusion.2
  293.7 0.0 copy-start.6
  293.8 0.5 fusion.16
  294.3 0.1 copy-done.6
  294.4 0.4 copy-done.4
  294.8 1.6 fusion
  296.4 0.0 reduce-scatter.2.cloned.1.call-update
  296.5 0.6 copy-done.11
  297.1 0.1 add.85
  297.2 0.0 copy-start.7
  297.2 1.6 convolution_bitcast_fusion.2
  298.8 30.0 %reduce-scatter.2.cloned.1.call-done = bf16[320,256]{1,0:T(8,128)(2,1)} async-done(((bf16[320,2048]{1,0:T(8,128)(2,1)}), bf16[320,256]{1,0:T(8,128)(2,1)}) %reduce-scatter.2.cloned.1.call-update) | async-done | bytes 163856 | tf_op jit(solution)/shard_map/reduce_scatter | solution.py:106
  328.8 1.7 all_to_all.85
  330.5 14.4 %all-to-all-start.8 = ((bf16[64,5,256]{2,1,0:T(8,128)(2,1)}), bf16[64,5,256]{2,1,0:T(8,128)(2,1)S(1)}, u32[]{:S(2)}, u32[]{:S(2)}) async-start(bf16[64,5,256]{2,1,0:T(8,128)(2,1)} %all_to_all.85), calls=%async_computation.9 | async-start | bytes 524288 | tf_op jit(solution)/shard_map/all_to_all | solution.py:109
  345.0 1.6 convolution_bitcast_fusion.1
  346.6 1.6 convolution_bitcast_fusion
  348.2 8.8 %all-to-all-done.8 = bf16[64,5,256]{2,1,0:T(8,128)(2,1)S(1)} async-done(((bf16[64,5,256]{2,1,0:T(8,128)(2,1)}), bf16[64,5,256]{2,1,0:T(8,128)(2,1)S(1)}, u32[]{:S(2)}, u32[]{:S(2)}) %all-to-all-start.8) | async-done | bytes 163872 | tf_op jit(solution)/shard_map/all_to_all | solution.py:109
  357.0 0.1 reshape.177
  357.1 1.0 gather_fusion
  358.0 0.8 fusion.4
  (41 shorter events, 0.2 us)
Async XLA Ops:
  7.2 29.1 %copy-start.5 = (bf16[1,2048,128]{2,1,0:T(8,128)(2,1)S(1)}, bf16[1,2048,128]{2,1,0:T(8,128)(2,1)}, u32[]{:S(2)}) copy-start(bf16[1,2048,128]{2,1,0:T(8,128)(2,1)} %param.17) | copy-start | bytes 1572868
  36.3 29.8 %copy-start.12 = (s32[32,8]{0,1:T(8,128)S(1)}, s32[32,8]{0,1:T(8,128)}, u32[]{:S(2)}) copy-start(s32[32,8]{0,1:T(8,128)} %param.14) | copy-start | bytes 3076
  36.3 30.1 %copy-start.16 = (s32[64]{0:T(128)S(1)}, s32[64]{0:T(128)}, u32[]{:S(2)}) copy-start(s32[64]{0:T(128)} %param.16) | copy-start | bytes 772
  59.8 23.6 %all-to-all-start.1 = ((bf16[1,64,32,128]{3,2,0,1:T(8,128)(2,1)}), bf16[1,64,32,128]{3,2,0,1:T(8,128)(2,1)S(1)}, u32[]{:S(2)}, u32[]{:S(2)}) async-start(bf16[1,64,32,128]{3,2,0,1:T(8,128)(2,1)} %bitcast.3), calls=%async_computation.1 | async-start | bytes 1048576 | tf_op jit(solution)/shard_map/all_to_all | solution.py:14
  85.4 7.3 %copy-start.8 = (bf16[32,256]{1,0:T(8,128)(2,1)S(1)}, bf16[32,256]{1,0:T(8,128)(2,1)}, u32[]{:S(2)}) copy-start(bf16[32,256]{1,0:T(8,128)(2,1)} %param.12) | copy-start | bytes 49156
  85.4 35.5 %all-to-all-start.7 = ((bf16[1,64,32,128]{3,2,0,1:T(8,128)(2,1)}), bf16[1,64,32,128]{3,2,0,1:T(8,128)(2,1)S(1)}, u32[]{:S(2)}, u32[]{:S(2)}) async-start(bf16[1,64,32,128]{3,2,0,1:T(8,128)(2,1)} %get-tuple-element.11), calls=%async_computation.7 | async-start | bytes 1048576 | tf_op jit(solution)/shard_map/all_to_all | solution.py:12
  118.9 0.6 copy-start.10
  119.5 64.5 %copy-start.14 = (s32[256,1]{0,1:T(1,128)}, s32[256,1]{0,1:T(1,128)S(1)}, u32[]{:S(2)}) copy-start(s32[256,1]{0,1:T(1,128)S(1)} %compare_select_fusion.1) | copy-start | bytes 3076
  120.9 15.2 %copy-start = (bf16[1,64,32,128]{3,2,0,1:T(8,128)(2,1)}, bf16[1,64,32,128]{3,2,0,1:T(8,128)(2,1)S(1)}, u32[]{:S(2)}) copy-start(bf16[1,64,32,128]{3,2,0,1:T(8,128)(2,1)S(1)} %all-to-all-done.7) | copy-start | bytes 1572868
  120.9 32.5 %all-to-all-start.5 = ((bf16[1,64,32,128]{3,2,0,1:T(8,128)(2,1)}), bf16[1,64,32,128]{3,2,0,1:T(8,128)(2,1)S(1)}, u32[]{:S(2)}, u32[]{:S(2)}) async-start(bf16[1,64,32,128]{3,2,0,1:T(8,128)(2,1)} %get-tuple-element.10), calls=%async_computation.5 | async-start | bytes 1048576 | tf_op jit(solution)/shard_map/all_to_all | solution.py:13
  140.4 20.1 %copy-start.9 = (bf16[32,256]{1,0:T(8,128)(2,1)S(1)}, bf16[32,256]{1,0:T(8,128)(2,1)}, u32[]{:S(2)}) copy-start(bf16[32,256]{1,0:T(8,128)(2,1)} %param.13) | copy-start | bytes 49156
  153.4 0.8 copy-start.2
  154.2 57.5 %all-to-all-start.3 = ((bf16[64,5,2048]{2,1,0:T(8,128)(2,1)}), bf16[64,5,2048]{2,1,0:T(8,128)(2,1)S(1)}, u32[]{:S(2)}, u32[]{:S(2)}) async-start(bf16[64,5,2048]{2,1,0:T(8,128)(2,1)} %all_to_all.76), calls=%async_computation.3 | async-start | bytes 4194304 | tf_op jit(solution)/shard_map/all_to_all | solution.py:99
  180.8 3.0 copy-start.13
  268.9 23.3 %all-to-all-start.2 = ((bf16[1,64,32,128]{3,2,0,1:T(8,128)(2,1)}), bf16[1,64,32,128]{3,2,0,1:T(8,128)(2,1)}, u32[]{:S(2)}, u32[]{:S(2)}) async-start(bf16[1,64,32,128]{3,2,0,1:T(8,128)(2,1)} %get-tuple-element.12), calls=%async_computation.2 | async-start | bytes 1048576 | tf_op jit(solution)/shard_map/all_to_all | solution.py:14
  274.9 53.9 %reduce-scatter.2.cloned.1.call-start = ((), (), s32[]{:S(2)}) async-start(), calls=%async_computation.10 | async-start | bytes 1474560 | tf_op jit(solution)/shard_map/reduce_scatter | solution.py:106
  275.6 2.7 copy-start.1
  278.2 1.0 copy-start.3
  293.7 0.6 copy-start.6
  293.7 1.1 copy-start.4
  296.4 0.7 copy-start.11
  296.4 0.7 copy-start.15
  297.2 47.8 %copy-start.7 = (bf16[320,128]{1,0:T(8,128)(2,1)S(1)}, bf16[320,128]{1,0:T(8,128)(2,1)}, u32[]{:S(2)}) copy-start(bf16[320,128]{1,0:T(8,128)(2,1)} %copy-done.6) | copy-start | bytes 245764
  330.5 26.4 %all-to-all-start.8 = ((bf16[64,5,256]{2,1,0:T(8,128)(2,1)}), bf16[64,5,256]{2,1,0:T(8,128)(2,1)S(1)}, u32[]{:S(2)}, u32[]{:S(2)}) async-start(bf16[64,5,256]{2,1,0:T(8,128)(2,1)} %all_to_all.85), calls=%async_computation.9 | async-start | bytes 524288 | tf_op jit(solution)/shard_map/all_to_all | solution.py:109
Sparse Core Ops, SparseCore 0:
  296.6 32.2 reduce-scatter.1
where the time goes:
time: 367 us; the launch traced here: 366 us
  blocking collectives  156 us (43%)
  waiting for transfers between devices  103 us (28%)
  starting transfers between devices  54.6 us (15%)
  local copies, waits for them, and re-layouts  23.3 us (6%)
  between operations  14.4 us (4%)
  matrix products  9.48 us (3%)
  other arithmetic  4.82 us (1%)
    all_to_all x1, blocking collectives, local(): lax.all_to_all(grads, 'expert', split_axis=0, concat_axis=0, tiled=True)  57.2 us
    reduce_scatter x1, waiting for transfers between devices, local(): lax.psum_scatter(partial_value, 'dp', scatter_dimension=1, tiled=True)  30 us
    all_to_all x1, blocking collectives, relay_weights(): lax.all_to_all(second, 'expert', split_axis=1, concat_axis=0, tiled=True)  29.1 us
    all_to_all x2, waiting for transfers between devices, relay_weights(): lax.all_to_all(third, 'expert', split_axis=1, concat_axis=0, tiled=True)  28.1 us
    all_gather x1, blocking collectives, local(): lax.all_gather(tokens, 'dp', axis=1, tiled=True)  26.1 us
    all_to_all x1, blocking collectives, relay_weights(): lax.all_to_all(first, 'expert', split_axis=1, concat_axis=0, tiled=True)  23.5 us
    all_to_all x1, waiting for transfers between devices, local(): lax.all_to_all(inputs, 'expert', split_axis=0, concat_axis=0, tiled=True)  22.9 us
    all_gather x1, blocking collectives, local(): lax.all_gather(cotangent, 'dp', axis=1, tiled=True)  20.2 us
  transfers between devices with their start and end apart: 7, of which 6 were waited for; matrix products, arithmetic and copies ran while one was open for 5% of the time, Pallas kernels for 0%

commit v1 on v0

--- a/solution.py
+++ b/solution.py
@@ -1,3 +1,4 @@
+import functools
 import jax
 import jax.numpy as jnp
 from jax import lax
@@ -5,6 +6,21 @@
 
 contract_rows = (((0,), (0,)), ((), ()))
 contract_cols = (((1,), (1,)), ((), ()))
+
+
+def pair_the_positions(xin, which_axis, dimension_no):
+    n_all = lax.psum(1, which_axis)
+    heap = tuple((n_all if t == dimension_no else 1 for t in range(xin.ndim)))
+    return lax.all_to_all(
+        jnp.tile(xin, heap),
+        axis_name=which_axis,
+        split_axis=dimension_no,
+        concat_axis=dimension_no,
+        tiled=True,
+    )
+
+
+map_ends = functools.partial(pair_the_positions, which_axis="dp", dimension_no=1)
 
 
 def relay_weights(first, second, third):
@@ -90,10 +106,7 @@
     hidden_width = gate_weight.shape[2]
     w_gate, w_up, w_down = migrate((gate_weight, up_weight, down_weight), matching, relay_weights)
     slot, slot_token, slot_prob = layout(routes, probs, matching, capacity)
-    whole_in, whole_out = (
-        lax.all_gather(tokens, "dp", axis=1, tiled=True),
-        lax.all_gather(cotangent, "dp", axis=1, tiled=True),
-    )
+    whole_in, whole_out = (map_ends(tokens), lax.all_gather(cotangent, "dp", axis=1, tiled=True))
     inputs, grads = build_rows(whole_in, whole_out, slot_token, slot_prob)
     arrived_in, arrived_out = (
         lax.all_to_all(inputs, "expert", split_axis=0, concat_axis=0, tiled=True),

time: 367 us -> 377 us (1.027)
  blocking collectives: 156 us -> 129 us
  waiting for transfers between devices: 103 us -> 128 us
  starting transfers between devices: 54.6 us -> 66.3 us
    all_to_all x1 -> x2, waiting for transfers between devices: 22.9 us -> 51 us  [the longest x1 45.1 us: local(): lax.all_to_all(grads, 'expert', split_axis=0, concat_axis=0, tiled=True)]
    all_gather x1 -> x0, blocking collectives: 26.1 us -> none  [local(): lax.all_gather(tokens, 'dp', axis=1, tiled=True)]
    all_to_all x1 -> x2, starting transfers between devices: 6.28 us -> 16.3 us  [the longest x1 10 us: pair_the_positions(): lax.all_to_all(jnp.tile(xin, heap), axis_name=which_axis, split_axis=dime...]
  transfers between devices with their start and end apart: 7 -> 8, of which waited for: 6 -> 7; matrix products, arithmetic and copies ran while one was open for 5% -> 6% of each run, Pallas kernels for 0% -> 0%
where the time goes in v1:
time: 377 us; the launch traced here: 376 us
  blocking collectives  129 us (34%)
  waiting for transfers between devices  128 us (34%)
  starting transfers between devices  66.3 us (18%)
  local copies, waits for them, and re-layouts  23.3 us (6%)
  between operations  14.5 us (4%)
  matrix products  9.46 us (3%)
  other arithmetic  4.82 us (1%)
    all_to_all x1, blocking collectives, local(): lax.all_to_all(inputs, 'expert', split_axis=0, concat_axis=0, tiled=True)  57.2 us
    all_to_all x1, waiting for transfers between devices, local(): lax.all_to_all(grads, 'expert', split_axis=0, concat_axis=0, tiled=True)  45.1 us
    all_to_all x1, blocking collectives, relay_weights(): lax.all_to_all(second, 'expert', split_axis=1, concat_axis=0, tiled=True)  29.1 us
    reduce_scatter x1, waiting for transfers between devices, local(): lax.psum_scatter(partial_value, 'dp', scatter_dimension=1, tiled=True)  28.8 us
    all_to_all x2, waiting for transfers between devices, relay_weights(): lax.all_to_all(third, 'expert', split_axis=1, concat_axis=0, tiled=True)  28.1 us
    all_to_all x1, blocking collectives, relay_weights(): lax.all_to_all(first, 'expert', split_axis=1, concat_axis=0, tiled=True)  23.5 us
    all_gather x1, blocking collectives, local(): lax.all_gather(cotangent, 'dp', axis=1, tiled=True)  19.7 us
    all_to_all x1, starting transfers between devices, relay_weights(): lax.all_to_all(second, 'expert', split_axis=1, concat_axis=0, tiled=True)  15.2 us
  transfers between devices with their start and end apart: 8, of which 7 were waited for; matrix products, arithmetic and copies ran while one was open for 6% of the time, Pallas kernels for 0%

profile of v1, /device:TPU:1, one launch (start us, length us, event | category | flops | bytes accessed | tf_op | source)
XLA Modules:
  0.0 375.9 jit_solution(1189057560015589617)
XLA Ops:
  7.2 29.1 %all_to_all.105 = bf16[1,64,32,128]{3,2,0,1:T(8,128)(2,1)S(1)} all-to-all(bf16[1,64,32,128]{3,2,0,1:T(8,128)(2,1)} %bitcast.87), channel_id=1, replica_groups=mesh['dp'=8,'expert'=64] {'expert'}, dimensions={1} | all-to-all | bytes 1048576 | tf_op jit(solution)/shard_map/all_to_all | solution.py:29
  36.3 23.5 %all_to_all.106 = bf16[1,64,32,128]{3,2,0,1:T(8,128)(2,1)S(1)} all-to-all(bf16[1,64,32,128]{3,2,0,1:T(8,128)(2,1)S(1)} %bitcast.88), channel_id=1, replica_groups=mesh['dp'=8,'expert'=64] {'expert'}, dimensions={1} | all-to-all | bytes 1048576 | tf_op jit(solution)/shard_map/all_to_all | solution.py:28
  59.8 6.3 %all-to-all-start.1 = ((bf16[1,64,32,128]{3,2,0,1:T(8,128)(2,1)}), bf16[1,64,32,128]{3,2,0,1:T(8,128)(2,1)S(1)}, u32[]{:S(2)}, u32[]{:S(2)}) async-start(bf16[1,64,32,128]{3,2,0,1:T(8,128)(2,1)} %bitcast.3), calls=%async_computation.1 | async-start | bytes 1048576 | tf_op jit(solution)/shard_map/all_to_all | solution.py:30
  66.1 0.0 copy-start.8
  66.1 0.1 copy.16
  66.2 0.1 eq.25
  66.3 0.1 eq.29
  66.4 0.7 gather_fusion.4
  67.1 0.7 gather_fusion.5
  67.7 15.7 %all-to-all-done.1 = bf16[1,64,32,128]{3,2,0,1:T(8,128)(2,1)S(1)} async-done(((bf16[1,64,32,128]{3,2,0,1:T(8,128)(2,1)}), bf16[1,64,32,128]{3,2,0,1:T(8,128)(2,1)S(1)}, u32[]{:S(2)}, u32[]{:S(2)}) %all-to-all-start.1) | async-done | bytes 524320 | tf_op jit(solution)/shard_map/all_to_all | solution.py:30
  83.4 0.7 tile.2
  84.1 10.0 %all-to-all-start.3 = ((bf16[32,8,256]{2,0,1:T(8,128)(2,1)}), bf16[32,8,256]{2,0,1:T(8,128)(2,1)S(1)}, u32[]{:S(2)}, u32[]{:S(2)}) async-start(bf16[32,8,256]{2,0,1:T(8,128)(2,1)} %tile.2), calls=%async_computation.3 | async-start | bytes 262144 | tf_op jit(solution)/shard_map/all_to_all | solution.py:14
  94.1 0.7 gather_fusion.2
  94.8 1.4 fusion.2
  96.1 6.0 %all-to-all-done.3 = bf16[32,8,256]{2,0,1:T(8,128)(2,1)S(1)} async-done(((bf16[32,8,256]{2,0,1:T(8,128)(2,1)}), bf16[32,8,256]{2,0,1:T(8,128)(2,1)S(1)}, u32[]{:S(2)}, u32[]{:S(2)}) %all-to-all-start.3) | async-done | bytes 131104 | tf_op jit(solution)/shard_map/all_to_all | solution.py:14
  102.1 7.7 %all-to-all-start.8 = ((bf16[1,64,32,128]{3,2,0,1:T(8,128)(2,1)}), bf16[1,64,32,128]{3,2,0,1:T(8,128)(2,1)S(1)}, u32[]{:S(2)}, u32[]{:S(2)}) async-start(bf16[1,64,32,128]{3,2,0,1:T(8,128)(2,1)} %get-tuple-element.11), calls=%async_computation.8 | async-start | bytes 1048576 | tf_op jit(solution)/shard_map/all_to_all | solution.py:28
  109.8 0.6 reduce-window.6
  110.4 0.2 slice_reduce_fusion
  110.6 0.1 copy.19
  110.7 0.1 reshape.251
  110.8 19.7 %all_gather.3 = bf16[32,2048]{1,0:T(8,128)(2,1)S(1)} all-gather(bf16[32,256]{1,0:T(8,128)(2,1)S(1)} %copy-done.9), channel_id=1, replica_groups=mesh['dp'=8,'expert'=64] {'dp'}, dimensions={1}, use_global_device_ids=true | all-gather | bytes 147456 | tf_op jit(solution)/shard_map/all_gather | solution.py:109
  130.5 0.1 select_reduce_fusion
  130.6 0.0 copy-start.14
  130.7 1.4 scatter_custom_fusion
  132.1 0.0 copy-start
  132.1 15.2 %all-to-all-start.6 = ((bf16[1,64,32,128]{3,2,0,1:T(8,128)(2,1)}), bf16[1,64,32,128]{3,2,0,1:T(8,128)(2,1)S(1)}, u32[]{:S(2)}, u32[]{:S(2)}) async-start(bf16[1,64,32,128]{3,2,0,1:T(8,128)(2,1)} %get-tuple-element.10), calls=%async_computation.6 | async-start | bytes 1048576 | tf_op jit(solution)/shard_map/all_to_all | solution.py:29
  147.4 2.4 gather_fusion.1
  149.8 1.4 scatter_custom_fusion.1
  151.2 0.4 multiply_convert_fusion
  151.6 1.6 all_to_all.76
  153.2 11.4 %all-to-all-done.6 = bf16[1,64,32,128]{3,2,0,1:T(8,128)(2,1)S(1)} async-done(((bf16[1,64,32,128]{3,2,0,1:T(8,128)(2,1)}), bf16[1,64,32,128]{3,2,0,1:T(8,128)(2,1)S(1)}, u32[]{:S(2)}, u32[]{:S(2)}) %all-to-all-start.6) | async-done | bytes 524320 | tf_op jit(solution)/shard_map/all_to_all | solution.py:29
  164.6 0.8 copy-done.2
  165.4 6.3 %all-to-all-start = ((bf16[64,5,2048]{2,1,0:T(8,128)(2,1)}), bf16[64,5,2048]{2,1,0:T(8,128)(2,1)S(1)}, u32[]{:S(2)}, u32[]{:S(2)}) async-start(bf16[64,5,2048]{2,1,0:T(8,128)(2,1)} %all_to_all.76), calls=%async_computation | async-start | bytes 4194304 | tf_op jit(solution)/shard_map/all_to_all | solution.py:113
  171.8 3.0 gather_fusion.3
  174.8 1.5 broadcast_select_fusion
  176.3 1.6 all_to_all.84
  177.9 45.1 %all-to-all-done = bf16[64,5,2048]{2,1,0:T(8,128)(2,1)S(1)} async-done(((bf16[64,5,2048]{2,1,0:T(8,128)(2,1)}), bf16[64,5,2048]{2,1,0:T(8,128)(2,1)S(1)}, u32[]{:S(2)}, u32[]{:S(2)}) %all-to-all-start) | async-done | bytes 1310752 | tf_op jit(solution)/shard_map/all_to_all | solution.py:113
  223.0 57.2 %all_to_all.107 = bf16[64,5,2048]{2,1,0:T(8,128)(2,1)} all-to-all(bf16[64,5,2048]{2,1,0:T(8,128)(2,1)} %all_to_all.84), channel_id=1, replica_groups=mesh['dp'=8,'expert'=64] {'expert'}, dimensions={0} | all-to-all | bytes 2621440 | tf_op jit(solution)/shard_map/all_to_all | solution.py:112
  280.1 6.0 %all-to-all-start.2 = ((bf16[1,64,32,128]{3,2,0,1:T(8,128)(2,1)}), bf16[1,64,32,128]{3,2,0,1:T(8,128)(2,1)}, u32[]{:S(2)}, u32[]{:S(2)}) async-start(bf16[1,64,32,128]{3,2,0,1:T(8,128)(2,1)} %get-tuple-element.12), calls=%async_computation.2 | async-start | bytes 1048576 | tf_op jit(solution)/shard_map/all_to_all | solution.py:30
  286.2 0.0 reduce-scatter.2.cloned.1.call-start
  286.2 0.6 all_to_all.78
  286.8 2.6 all_to_all.86
  289.5 0.5 fusion.15
  290.0 0.5 copy-done.3
  290.5 0.5 fusion.14
  291.0 12.4 %all-to-all-done.2 = bf16[1,64,32,128]{3,2,0,1:T(8,128)(2,1)} async-done(((bf16[1,64,32,128]{3,2,0,1:T(8,128)(2,1)}), bf16[1,64,32,128]{3,2,0,1:T(8,128)(2,1)}, u32[]{:S(2)}, u32[]{:S(2)}) %all-to-all-start.2) | async-done | bytes 524320 | tf_op jit(solution)/shard_map/all_to_all | solution.py:30
  303.4 1.5 multiply_convert_fusion.2
  305.0 0.5 fusion.16
  305.5 0.1 copy-done.6
  305.6 0.4 copy-done.4
  306.0 1.6 fusion
  307.6 0.0 reduce-scatter.2.cloned.1.call-update
  307.7 0.7 copy-done.11
  308.3 0.1 add.85
  308.4 1.6 convolution_bitcast_fusion.2
  310.0 28.8 %reduce-scatter.2.cloned.1.call-done = bf16[320,256]{1,0:T(8,128)(2,1)} async-done(((bf16[320,2048]{1,0:T(8,128)(2,1)}), bf16[320,256]{1,0:T(8,128)(2,1)}) %reduce-scatter.2.cloned.1.call-update) | async-done | bytes 163856 | tf_op jit(solution)/shard_map/reduce_scatter | solution.py:119
  338.8 1.7 all_to_all.93
  340.5 14.7 %all-to-all-start.9 = ((bf16[64,5,256]{2,1,0:T(8,128)(2,1)}), bf16[64,5,256]{2,1,0:T(8,128)(2,1)S(1)}, u32[]{:S(2)}, u32[]{:S(2)}) async-start(bf16[64,5,256]{2,1,0:T(8,128)(2,1)} %all_to_all.93), calls=%async_computation.10 | async-start | bytes 524288 | tf_op jit(solution)/shard_map/all_to_all | solution.py:122
  355.3 1.6 convolution_bitcast_fusion.1
  356.9 1.6 convolution_bitcast_fusion
  358.5 8.8 %all-to-all-done.9 = bf16[64,5,256]{2,1,0:T(8,128)(2,1)S(1)} async-done(((bf16[64,5,256]{2,1,0:T(8,128)(2,1)}), bf16[64,5,256]{2,1,0:T(8,128)(2,1)S(1)}, u32[]{:S(2)}, u32[]{:S(2)}) %all-to-all-start.9) | async-done | bytes 163872 | tf_op jit(solution)/shard_map/all_to_all | solution.py:122
  367.3 0.1 reshape.184
  367.3 1.0 gather_fusion
  368.3 0.8 fusion.4
  (44 shorter events, 0.2 us)
Async XLA Ops:
  7.2 29.1 %copy-start.5 = (bf16[1,2048,128]{2,1,0:T(8,128)(2,1)S(1)}, bf16[1,2048,128]{2,1,0:T(8,128)(2,1)}, u32[]{:S(2)}) copy-start(bf16[1,2048,128]{2,1,0:T(8,128)(2,1)} %param.17) | copy-start | bytes 1572868
  36.3 29.8 %copy-start.12 = (s32[32,8]{0,1:T(8,128)S(1)}, s32[32,8]{0,1:T(8,128)}, u32[]{:S(2)}) copy-start(s32[32,8]{0,1:T(8,128)} %param.14) | copy-start | bytes 3076
  36.3 30.1 %copy-start.16 = (s32[64]{0:T(128)S(1)}, s32[64]{0:T(128)}, u32[]{:S(2)}) copy-start(s32[64]{0:T(128)} %param.16) | copy-start | bytes 772
  59.8 23.6 %all-to-all-start.1 = ((bf16[1,64,32,128]{3,2,0,1:T(8,128)(2,1)}), bf16[1,64,32,128]{3,2,0,1:T(8,128)(2,1)S(1)}, u32[]{:S(2)}, u32[]{:S(2)}) async-start(bf16[1,64,32,128]{3,2,0,1:T(8,128)(2,1)} %bitcast.3), calls=%async_computation.1 | async-start | bytes 1048576 | tf_op jit(solution)/shard_map/all_to_all | solution.py:30
  66.1 17.3 %copy-start.8 = (bf16[32,256]{1,0:T(8,128)(2,1)S(1)}, bf16[32,256]{1,0:T(8,128)(2,1)}, u32[]{:S(2)}) copy-start(bf16[32,256]{1,0:T(8,128)(2,1)} %param.12) | copy-start | bytes 49156
  84.1 18.0 %all-to-all-start.3 = ((bf16[32,8,256]{2,0,1:T(8,128)(2,1)}), bf16[32,8,256]{2,0,1:T(8,128)(2,1)S(1)}, u32[]{:S(2)}, u32[]{:S(2)}) async-start(bf16[32,8,256]{2,0,1:T(8,128)(2,1)} %tile.2), calls=%async_computation.3 | async-start | bytes 262144 | tf_op jit(solution)/shard_map/all_to_all | solution.py:14
  96.1 14.5 %copy-start.13 = (f32[32,8]{0,1:T(8,128)S(1)}, f32[32,8]{0,1:T(8,128)}, u32[]{:S(2)}) copy-start(f32[32,8]{0,1:T(8,128)} %param.15) | copy-start | bytes 3076
  96.1 14.7 %copy-start.9 = (bf16[32,256]{1,0:T(8,128)(2,1)S(1)}, bf16[32,256]{1,0:T(8,128)(2,1)}, u32[]{:S(2)}) copy-start(bf16[32,256]{1,0:T(8,128)(2,1)} %param.13) | copy-start | bytes 49156
  102.1 30.0 %all-to-all-start.8 = ((bf16[1,64,32,128]{3,2,0,1:T(8,128)(2,1)}), bf16[1,64,32,128]{3,2,0,1:T(8,128)(2,1)S(1)}, u32[]{:S(2)}, u32[]{:S(2)}) async-start(bf16[1,64,32,128]{3,2,0,1:T(8,128)(2,1)} %get-tuple-element.11), calls=%async_computation.8 | async-start | bytes 1048576 | tf_op jit(solution)/shard_map/all_to_all | solution.py:28
  130.6 16.7 %copy-start.10 = (s32[256]{0:T(256)}, s32[256]{0:T(256)S(1)}, u32[]{:S(2)}) copy-start(s32[256]{0:T(256)S(1)} %add_add_fusion) | copy-start | bytes 3076
  130.6 19.2 %copy-start.14 = (s32[256,1]{0,1:T(1,128)}, s32[256,1]{0,1:T(1,128)S(1)}, u32[]{:S(2)}) copy-start(s32[256,1]{0,1:T(1,128)S(1)} %compare_select_fusion.1) | copy-start | bytes 3076
  132.1 15.3 %copy-start = (bf16[1,64,32,128]{3,2,0,1:T(8,128)(2,1)}, bf16[1,64,32,128]{3,2,0,1:T(8,128)(2,1)S(1)}, u32[]{:S(2)}) copy-start(bf16[1,64,32,128]{3,2,0,1:T(8,128)(2,1)S(1)} %all-to-all-done.8) | copy-start | bytes 1572868
  132.1 32.6 %all-to-all-start.6 = ((bf16[1,64,32,128]{3,2,0,1:T(8,128)(2,1)}), bf16[1,64,32,128]{3,2,0,1:T(8,128)(2,1)S(1)}, u32[]{:S(2)}, u32[]{:S(2)}) async-start(bf16[1,64,32,128]{3,2,0,1:T(8,128)(2,1)} %get-tuple-element.10), calls=%async_computation.6 | async-start | bytes 1048576 | tf_op jit(solution)/shard_map/all_to_all | solution.py:29
  164.6 0.8 copy-start.2
  165.4 57.5 %all-to-all-start = ((bf16[64,5,2048]{2,1,0:T(8,128)(2,1)}), bf16[64,5,2048]{2,1,0:T(8,128)(2,1)S(1)}, u32[]{:S(2)}, u32[]{:S(2)}) async-start(bf16[64,5,2048]{2,1,0:T(8,128)(2,1)} %all_to_all.76), calls=%async_computation | async-start | bytes 4194304 | tf_op jit(solution)/shard_map/all_to_all | solution.py:113
  280.1 23.3 %all-to-all-start.2 = ((bf16[1,64,32,128]{3,2,0,1:T(8,128)(2,1)}), bf16[1,64,32,128]{3,2,0,1:T(8,128)(2,1)}, u32[]{:S(2)}, u32[]{:S(2)}) async-start(bf16[1,64,32,128]{3,2,0,1:T(8,128)(2,1)} %get-tuple-element.12), calls=%async_computation.2 | async-start | bytes 1048576 | tf_op jit(solution)/shard_map/all_to_all | solution.py:30
  286.2 52.7 %reduce-scatter.2.cloned.1.call-start = ((), (), s32[]{:S(2)}) async-start(), calls=%async_computation.11 | async-start | bytes 1474560 | tf_op jit(solution)/shard_map/reduce_scatter | solution.py:119
  286.8 2.7 copy-start.1
  289.4 1.0 copy-start.3
  304.9 0.6 copy-start.6
  305.0 1.1 copy-start.4
  307.6 0.7 copy-start.11
  307.6 0.8 copy-start.15
  308.4 46.8 %copy-start.7 = (bf16[320,128]{1,0:T(8,128)(2,1)S(1)}, bf16[320,128]{1,0:T(8,128)(2,1)}, u32[]{:S(2)}) copy-start(bf16[320,128]{1,0:T(8,128)(2,1)} %copy-done.6) | copy-start | bytes 245764
  340.5 26.8 %all-to-all-start.9 = ((bf16[64,5,256]{2,1,0:T(8,128)(2,1)}), bf16[64,5,256]{2,1,0:T(8,128)(2,1)S(1)}, u32[]{:S(2)}, u32[]{:S(2)}) async-start(bf16[64,5,256]{2,1,0:T(8,128)(2,1)} %all_to_all.93), calls=%async_computation.10 | async-start | bytes 524288 | tf_op jit(solution)/shard_map/all_to_all | solution.py:122
Sparse Core Ops, SparseCore 0:
  307.8 30.9 reduce-scatter.1
